TPU v7x, 128 devices: a whole 4x4x4 slice. The times are simulated.
128 devices in a mesh: row: 8 (over x, y_lo), col: 16 (over y_hi, z, core).
Axes of the slice: x: 4, y: 4 (y_hi: 2, y_lo: 2; y = y_hi * 2 + y_lo), z: 4, core: 2. Of those that a mesh axis runs over, the one named last changes fastest.
Arguments:
- gradients: bfloat16 [3, 8, 256, 64, 128], P(None, 'row', 'col'), may hold values from -6 to 6
- tile_blocks: bfloat16 [49152, 128, 128], P(('row', 'col')), may hold values from -0.15625 to 0.15625
- tile_rows: int32 [49152], P(('row', 'col')), may hold values from 0 to 255
- tile_cols: int32 [49152], P(('row', 'col')), may hold values from 0 to 127
- tile_counts: int32 [128], P(('row', 'col')), may hold values from 48 to 384, as said below
Outputs:
- adjoint: bfloat16 [3, 16, 128, 64, 128], P(None, 'col', 'row')
Inputs may be any that keep to these rules, and one draw needn't show every extreme that they name: `tile_counts`: some device uses all 384 slots; slots from a device's count on add nothing.
All inputs are finite; a program needn't handle non-finite values.
Results may differ from a plain program's by a relative error of at most 0.011.
Values may be sent and summed in bfloat16 or wider, within the bound.
A program may use at most 128 MiB of HBM per device.

v0:
```python
import math

import jax
import jax.numpy as jnp
from jax import lax
from jax.sharding import PartitionSpec as P


def live_products(row_panel, tile_data, row_ids, col_ids, live_count, column_blocks):
    slot_count = tile_data.shape[0]
    row_blocks = row_panel.shape[1]
    group_size = math.gcd(slot_count, 64)
    acc_shape = (column_blocks, row_panel.shape[0], row_panel.shape[2], row_panel.shape[3])

    def advance(turn_index, running):
        offset = turn_index * group_size
        group_tiles = lax.dynamic_slice_in_dim(tile_data, offset, group_size, 0)
        group_rows = lax.dynamic_slice_in_dim(row_ids, offset, group_size, 0)
        group_cols = lax.dynamic_slice_in_dim(col_ids, offset, group_size, 0)
        alive_mask = offset + lax.iota(jnp.int32, group_size) < live_count
        row_onehot = (
            (group_rows[:, None] == lax.iota(jnp.int32, row_blocks)[None, :]) & alive_mask[:, None]
        ).astype(jnp.bfloat16)
        picked = jnp.einsum(
            "gr,srjp->sgjp", row_onehot, row_panel, preferred_element_type=jnp.float32
        ).astype(jnp.bfloat16)
        products_f = jnp.einsum(
            "sgjp,gpq->gsjq", picked, group_tiles, preferred_element_type=jnp.float32
        )
        upper_part = products_f.astype(jnp.bfloat16)
        lower_part = (products_f - upper_part.astype(jnp.float32)).astype(jnp.bfloat16)
        col_onehot = (lax.iota(jnp.int32, column_blocks)[:, None] == group_cols[None, :]).astype(
            jnp.bfloat16
        )
        added = jnp.einsum(
            "cg,gsjq->csjq", col_onehot, upper_part, preferred_element_type=jnp.float32
        )
        added = added + jnp.einsum(
            "cg,gsjq->csjq", col_onehot, lower_part, preferred_element_type=jnp.float32
        )
        return running + added

    turn_count = slot_count // group_size
    summed = lax.fori_loop(0, turn_count, advance, jnp.zeros(acc_shape, jnp.float32))
    return jnp.transpose(summed, (1, 0, 2, 3))


def shards(gradients, tile_blocks, tile_rows, tile_cols, tile_counts):
    live_count = tile_counts[0]
    column_blocks = gradients.shape[2] * lax.axis_size("row")
    own_blocks = gradients[:, 0]
    pieces = []
    for set_index in range(own_blocks.shape[0]):
        row_panel = lax.all_gather(own_blocks[set_index : set_index + 1], "col", axis=1, tiled=True)
        partial_value = live_products(
            row_panel, tile_blocks, tile_rows, tile_cols, live_count, column_blocks
        )
        owned_share = lax.psum_scatter(partial_value, "row", scatter_dimension=1, tiled=True)
        pieces.append(owned_share.astype(jnp.bfloat16))
    result = jnp.concatenate(pieces, 0)
    return result[:, None]


def solution(mesh):
    in_specs = (
        P(None, "row", "col", None, None),
        P(("row", "col"), None, None),
        P(("row", "col")),
        P(("row", "col")),
        P(("row", "col")),
    )
    out_specs = P(None, "col", "row", None, None)
    return jax.shard_map(shards, mesh=mesh, in_specs=in_specs, out_specs=out_specs, check_vma=False)
```

profile of v0, /device:TPU:0, one launch (start us, length us, event | category | flops | bytes accessed | tf_op | source)
XLA Modules:
  0.0 518.2 jit_solution(4917629098204719745)
XLA Ops:
  10.1 57.6 %all-gather.7.cloned.1.call-done = bf16[1,1,256,64,128]{4,3,1,0,2:T(8,128)(2,1)} async-done(((bf16[1,1,16,64,128]{4,3,1,0,2:T(8,128)(2,1)}), bf16[1,1,256,64,128]{4,3,1,0,2:T(8,128)(2,1)}) %all-gather.7.cloned.1.call-update) | async-done | bytes 4194320 | tf_op jit(solution)/shard_map/all_gather | solution.py:54
  67.8 116.7 %while.42 = (s32[]{:T(128)}, f32[128,1,64,128]{3,0,2,1:T(8,128)}, s32[384]{0:T(512)}, s32[384]{0:T(512)}, s32[]{:T(128)}, /*index=5*/bf16[1,256,64,128]{3,2,1,0:...) while((s32[]{:T(128)}, f32[128,1,64,128]{3,0,2,1:T(8,128)}, ...), condition=%wide.region_1.0_spmd.clone, body=%wide.region_0.0_spmd.clone.sunk | while | flops 676380800 | bytes 29362232 | solution.py:44
  80.5 5.5 %bitcast_add_fusion.6 = f32[128,1,64,128]{3,0,2,1:T(8,128)} fusion(f32[128,1,64,128]{3,0,2,1:T(8,128)} %get-tuple-element.722, f32[128,64,128]{2,0,1:T(8,128)} %fusion.85, pred[]{:T(512)S(6)} %compare.9, bf16[64,64,128]{2,1,0:T(8,128)(2,1)S(1)} %get-tuple-element.625, s32[64]{0:T(128)S(1)} %dynamic_slice.95), kind=kOutput, calls=%fused_computation.clone.1 | convolution fusion | flops 137371648 | bytes 13631745 | tf_op jit(solution)/shard_map/while/body/eval_jaxpr/cg,gsjq->csjq/dot_general | solution.py:38
  98.7 7.3 %bitcast_add_fusion.6 = f32[128,1,64,128]{3,0,2,1:T(8,128)} fusion(f32[128,1,64,128]{3,0,2,1:T(8,128)} %get-tuple-element.722, f32[128,64,128]{2,0,1:T(8,128)} %fusion.85, pred[]{:T(512)S(6)} %compare.9, bf16[64,64,128]{2,1,0:T(8,128)(2,1)S(1)} %get-tuple-element.625, s32[64]{0:T(128)S(1)} %dynamic_slice.95), kind=kOutput, calls=%fused_computation.clone.1 | convolution fusion | flops 137371648 | bytes 13631745 | tf_op jit(solution)/shard_map/while/body/eval_jaxpr/cg,gsjq->csjq/dot_general | solution.py:38
  118.8 6.9 %bitcast_add_fusion.6 = f32[128,1,64,128]{3,0,2,1:T(8,128)} fusion(f32[128,1,64,128]{3,0,2,1:T(8,128)} %get-tuple-element.722, f32[128,64,128]{2,0,1:T(8,128)} %fusion.85, pred[]{:T(512)S(6)} %compare.9, bf16[64,64,128]{2,1,0:T(8,128)(2,1)S(1)} %get-tuple-element.625, s32[64]{0:T(128)S(1)} %dynamic_slice.95), kind=kOutput, calls=%fused_computation.clone.1 | convolution fusion | flops 137371648 | bytes 13631745 | tf_op jit(solution)/shard_map/while/body/eval_jaxpr/cg,gsjq->csjq/dot_general | solution.py:38
  138.5 6.8 %bitcast_add_fusion.6 = f32[128,1,64,128]{3,0,2,1:T(8,128)} fusion(f32[128,1,64,128]{3,0,2,1:T(8,128)} %get-tuple-element.722, f32[128,64,128]{2,0,1:T(8,128)} %fusion.85, pred[]{:T(512)S(6)} %compare.9, bf16[64,64,128]{2,1,0:T(8,128)(2,1)S(1)} %get-tuple-element.625, s32[64]{0:T(128)S(1)} %dynamic_slice.95), kind=kOutput, calls=%fused_computation.clone.1 | convolution fusion | flops 137371648 | bytes 13631745 | tf_op jit(solution)/shard_map/while/body/eval_jaxpr/cg,gsjq->csjq/dot_general | solution.py:38
  158.0 6.8 %bitcast_add_fusion.6 = f32[128,1,64,128]{3,0,2,1:T(8,128)} fusion(f32[128,1,64,128]{3,0,2,1:T(8,128)} %get-tuple-element.722, f32[128,64,128]{2,0,1:T(8,128)} %fusion.85, pred[]{:T(512)S(6)} %compare.9, bf16[64,64,128]{2,1,0:T(8,128)(2,1)S(1)} %get-tuple-element.625, s32[64]{0:T(128)S(1)} %dynamic_slice.95), kind=kOutput, calls=%fused_computation.clone.1 | convolution fusion | flops 137371648 | bytes 13631745 | tf_op jit(solution)/shard_map/while/body/eval_jaxpr/cg,gsjq->csjq/dot_general | solution.py:38
  177.7 6.8 %bitcast_add_fusion.6 = f32[128,1,64,128]{3,0,2,1:T(8,128)} fusion(f32[128,1,64,128]{3,0,2,1:T(8,128)} %get-tuple-element.722, f32[128,64,128]{2,0,1:T(8,128)} %fusion.85, pred[]{:T(512)S(6)} %compare.9, bf16[64,64,128]{2,1,0:T(8,128)(2,1)S(1)} %get-tuple-element.625, s32[64]{0:T(128)S(1)} %dynamic_slice.95), kind=kOutput, calls=%fused_computation.clone.1 | convolution fusion | flops 137371648 | bytes 13631745 | tf_op jit(solution)/shard_map/while/body/eval_jaxpr/cg,gsjq->csjq/dot_general | solution.py:38
  184.5 6.6 %copy.71 = f32[128,1,64,128]{3,2,0,1:T(8,128)} copy(f32[128,1,64,128]{3,0,2,1:T(8,128)} %get-tuple-element.377) | data formatting | bytes 8388608 | tf_op jit(solution)/shard_map/while | solution.py:44
  191.8 108.2 %while.43 = (s32[]{:T(128)}, f32[128,1,64,128]{3,0,2,1:T(8,128)}, s32[384]{0:T(512)S(1)}, s32[384]{0:T(512)S(1)}, s32[]{:T(128)}, /*index=5*/bf16[1,256,64,128]{...) while((s32[]{:T(128)}, f32[128,1,64,128]{3,0,2,1:T(8,128)}, ...), condition=%wide.region_4.0_spmd.clone, body=%wide.region_3.0_spmd.clone.sunk | while | flops 676380800 | bytes 29362232 | solution.py:44
  203.3 5.5 %bitcast_add_fusion.7 = f32[128,1,64,128]{3,0,2,1:T(8,128)} fusion(f32[128,1,64,128]{3,0,2,1:T(8,128)} %get-tuple-element.689, f32[128,64,128]{2,0,1:T(8,128)} %fusion.93, pred[]{:T(512)S(6)} %compare.10, bf16[64,64,128]{2,1,0:T(8,128)(2,1)S(1)} %get-tuple-element.634, s32[64]{0:T(128)S(1)} %dynamic_slice.98), kind=kOutput, calls=%fused_computation.21.clone.1 | convolution fusion | flops 137371648 | bytes 13631745 | tf_op jit(solution)/shard_map/while/body/eval_jaxpr/cg,gsjq->csjq/dot_general | solution.py:38
  209.6 4.9 fusion.92
  220.3 6.8 %bitcast_add_fusion.7 = f32[128,1,64,128]{3,0,2,1:T(8,128)} fusion(f32[128,1,64,128]{3,0,2,1:T(8,128)} %get-tuple-element.689, f32[128,64,128]{2,0,1:T(8,128)} %fusion.93, pred[]{:T(512)S(6)} %compare.10, bf16[64,64,128]{2,1,0:T(8,128)(2,1)S(1)} %get-tuple-element.634, s32[64]{0:T(128)S(1)} %dynamic_slice.98), kind=kOutput, calls=%fused_computation.21.clone.1 | convolution fusion | flops 137371648 | bytes 13631745 | tf_op jit(solution)/shard_map/while/body/eval_jaxpr/cg,gsjq->csjq/dot_general | solution.py:38
  227.8 4.9 fusion.92
  238.5 6.8 %bitcast_add_fusion.7 = f32[128,1,64,128]{3,0,2,1:T(8,128)} fusion(f32[128,1,64,128]{3,0,2,1:T(8,128)} %get-tuple-element.689, f32[128,64,128]{2,0,1:T(8,128)} %fusion.93, pred[]{:T(512)S(6)} %compare.10, bf16[64,64,128]{2,1,0:T(8,128)(2,1)S(1)} %get-tuple-element.634, s32[64]{0:T(128)S(1)} %dynamic_slice.98), kind=kOutput, calls=%fused_computation.21.clone.1 | convolution fusion | flops 137371648 | bytes 13631745 | tf_op jit(solution)/shard_map/while/body/eval_jaxpr/cg,gsjq->csjq/dot_general | solution.py:38
  256.8 6.8 %bitcast_add_fusion.7 = f32[128,1,64,128]{3,0,2,1:T(8,128)} fusion(f32[128,1,64,128]{3,0,2,1:T(8,128)} %get-tuple-element.689, f32[128,64,128]{2,0,1:T(8,128)} %fusion.93, pred[]{:T(512)S(6)} %compare.10, bf16[64,64,128]{2,1,0:T(8,128)(2,1)S(1)} %get-tuple-element.634, s32[64]{0:T(128)S(1)} %dynamic_slice.98), kind=kOutput, calls=%fused_computation.21.clone.1 | convolution fusion | flops 137371648 | bytes 13631745 | tf_op jit(solution)/shard_map/while/body/eval_jaxpr/cg,gsjq->csjq/dot_general | solution.py:38
  264.3 4.9 fusion.92
  275.0 6.8 %bitcast_add_fusion.7 = f32[128,1,64,128]{3,0,2,1:T(8,128)} fusion(f32[128,1,64,128]{3,0,2,1:T(8,128)} %get-tuple-element.689, f32[128,64,128]{2,0,1:T(8,128)} %fusion.93, pred[]{:T(512)S(6)} %compare.10, bf16[64,64,128]{2,1,0:T(8,128)(2,1)S(1)} %get-tuple-element.634, s32[64]{0:T(128)S(1)} %dynamic_slice.98), kind=kOutput, calls=%fused_computation.21.clone.1 | convolution fusion | flops 137371648 | bytes 13631745 | tf_op jit(solution)/shard_map/while/body/eval_jaxpr/cg,gsjq->csjq/dot_general | solution.py:38
  293.2 6.8 %bitcast_add_fusion.7 = f32[128,1,64,128]{3,0,2,1:T(8,128)} fusion(f32[128,1,64,128]{3,0,2,1:T(8,128)} %get-tuple-element.689, f32[128,64,128]{2,0,1:T(8,128)} %fusion.93, pred[]{:T(512)S(6)} %compare.10, bf16[64,64,128]{2,1,0:T(8,128)(2,1)S(1)} %get-tuple-element.634, s32[64]{0:T(128)S(1)} %dynamic_slice.98), kind=kOutput, calls=%fused_computation.21.clone.1 | convolution fusion | flops 137371648 | bytes 13631745 | tf_op jit(solution)/shard_map/while/body/eval_jaxpr/cg,gsjq->csjq/dot_general | solution.py:38
  299.9 6.5 %copy.70 = f32[128,1,64,128]{3,2,0,1:T(8,128)} copy(f32[128,1,64,128]{3,0,2,1:T(8,128)} %get-tuple-element.378) | data formatting | bytes 8388608 | tf_op jit(solution)/shard_map/while | solution.py:44
  306.8 108.2 %while.44 = (s32[]{:T(128)}, f32[128,1,64,128]{3,0,2,1:T(8,128)}, s32[384]{0:T(512)S(1)}, s32[384]{0:T(512)S(1)}, s32[]{:T(128)}, /*index=5*/bf16[1,256,64,128]{...) while((s32[]{:T(128)}, f32[128,1,64,128]{3,0,2,1:T(8,128)}, ...), condition=%wide.region_7.0_spmd.clone, body=%wide.region_6.0_spmd.clone.sunk | while | flops 676380800 | bytes 29362232 | solution.py:44
  318.4 5.6 %bitcast_add_fusion.8 = f32[128,1,64,128]{3,0,2,1:T(8,128)} fusion(f32[128,1,64,128]{3,0,2,1:T(8,128)} %get-tuple-element.656, f32[128,64,128]{2,0,1:T(8,128)} %fusion.101, pred[]{:T(512)S(6)} %compare.11, bf16[64,64,128]{2,1,0:T(8,128)(2,1)S(1)} %get-tuple-element.643, s32[64]{0:T(128)S(1)} %dynamic_slice.101), kind=kOutput, calls=%fused_computation.42.clone.1 | convolution fusion | flops 137371648 | bytes 13631745 | tf_op jit(solution)/shard_map/while/body/eval_jaxpr/cg,gsjq->csjq/dot_general | solution.py:38
  324.7 4.9 fusion.100
  335.4 6.8 %bitcast_add_fusion.8 = f32[128,1,64,128]{3,0,2,1:T(8,128)} fusion(f32[128,1,64,128]{3,0,2,1:T(8,128)} %get-tuple-element.656, f32[128,64,128]{2,0,1:T(8,128)} %fusion.101, pred[]{:T(512)S(6)} %compare.11, bf16[64,64,128]{2,1,0:T(8,128)(2,1)S(1)} %get-tuple-element.643, s32[64]{0:T(128)S(1)} %dynamic_slice.101), kind=kOutput, calls=%fused_computation.42.clone.1 | convolution fusion | flops 137371648 | bytes 13631745 | tf_op jit(solution)/shard_map/while/body/eval_jaxpr/cg,gsjq->csjq/dot_general | solution.py:38
  342.9 4.9 fusion.100
  353.6 6.9 %bitcast_add_fusion.8 = f32[128,1,64,128]{3,0,2,1:T(8,128)} fusion(f32[128,1,64,128]{3,0,2,1:T(8,128)} %get-tuple-element.656, f32[128,64,128]{2,0,1:T(8,128)} %fusion.101, pred[]{:T(512)S(6)} %compare.11, bf16[64,64,128]{2,1,0:T(8,128)(2,1)S(1)} %get-tuple-element.643, s32[64]{0:T(128)S(1)} %dynamic_slice.101), kind=kOutput, calls=%fused_computation.42.clone.1 | convolution fusion | flops 137371648 | bytes 13631745 | tf_op jit(solution)/shard_map/while/body/eval_jaxpr/cg,gsjq->csjq/dot_general | solution.py:38
  371.8 6.8 %bitcast_add_fusion.8 = f32[128,1,64,128]{3,0,2,1:T(8,128)} fusion(f32[128,1,64,128]{3,0,2,1:T(8,128)} %get-tuple-element.656, f32[128,64,128]{2,0,1:T(8,128)} %fusion.101, pred[]{:T(512)S(6)} %compare.11, bf16[64,64,128]{2,1,0:T(8,128)(2,1)S(1)} %get-tuple-element.643, s32[64]{0:T(128)S(1)} %dynamic_slice.101), kind=kOutput, calls=%fused_computation.42.clone.1 | convolution fusion | flops 137371648 | bytes 13631745 | tf_op jit(solution)/shard_map/while/body/eval_jaxpr/cg,gsjq->csjq/dot_general | solution.py:38
  379.4 4.9 fusion.100
  390.0 6.8 %bitcast_add_fusion.8 = f32[128,1,64,128]{3,0,2,1:T(8,128)} fusion(f32[128,1,64,128]{3,0,2,1:T(8,128)} %get-tuple-element.656, f32[128,64,128]{2,0,1:T(8,128)} %fusion.101, pred[]{:T(512)S(6)} %compare.11, bf16[64,64,128]{2,1,0:T(8,128)(2,1)S(1)} %get-tuple-element.643, s32[64]{0:T(128)S(1)} %dynamic_slice.101), kind=kOutput, calls=%fused_computation.42.clone.1 | convolution fusion | flops 137371648 | bytes 13631745 | tf_op jit(solution)/shard_map/while/body/eval_jaxpr/cg,gsjq->csjq/dot_general | solution.py:38
  408.2 6.8 %bitcast_add_fusion.8 = f32[128,1,64,128]{3,0,2,1:T(8,128)} fusion(f32[128,1,64,128]{3,0,2,1:T(8,128)} %get-tuple-element.656, f32[128,64,128]{2,0,1:T(8,128)} %fusion.101, pred[]{:T(512)S(6)} %compare.11, bf16[64,64,128]{2,1,0:T(8,128)(2,1)S(1)} %get-tuple-element.643, s32[64]{0:T(128)S(1)} %dynamic_slice.101), kind=kOutput, calls=%fused_computation.42.clone.1 | convolution fusion | flops 137371648 | bytes 13631745 | tf_op jit(solution)/shard_map/while/body/eval_jaxpr/cg,gsjq->csjq/dot_general | solution.py:38
  415.0 6.6 %copy.69 = f32[128,1,64,128]{3,2,0,1:T(8,128)} copy(f32[128,1,64,128]{3,0,2,1:T(8,128)} %get-tuple-element.379) | data formatting | bytes 8388608 | tf_op jit(solution)/shard_map/while | solution.py:44
  423.9 85.5 %reduce-scatter.8.cloned.1.call-done = f32[1,16,64,128]{3,2,1,0:T(8,128)} async-done(((f32[1,128,64,128]{3,2,1,0:T(8,128)}), f32[1,16,64,128]{3,2,1,0:T(8,128)}) %reduce-scatter.8.cloned.1.call-update) | async-done | bytes 524304 | tf_op jit(solution)/shard_map/reduce_scatter | solution.py:58
  (130 shorter events, 193.0 us)
Async XLA Ops:
  6.5 61.2 %all-gather.7.cloned.1.call-start = ((), (), s32[]{:S(2)}) async-start(), calls=%async_computation.6 | async-start | bytes 4456448 | tf_op jit(solution)/shard_map/all_gather | solution.py:54
  8.6 182.8 %all-gather.9.cloned.1.call-start = ((), (), s32[]{:S(2)}) async-start(), calls=%async_computation.7 | async-start | bytes 4456448 | tf_op jit(solution)/shard_map/all_gather | solution.py:54
  9.3 297.5 %all-gather.11.cloned.1.call-start = ((), (), s32[]{:S(2)}) async-start(), calls=%async_computation.8 | async-start | bytes 4456448 | tf_op jit(solution)/shard_map/all_gather | solution.py:54
  10.1 411.6 %reduce-scatter.4.cloned.1.call-start = ((), (), s32[]{:S(2)}) async-start(), calls=%async_computation.3 | async-start | bytes 4718592 | tf_op jit(solution)/shard_map/reduce_scatter | solution.py:58
  191.1 0.7 copy-start
  191.1 0.7 copy-start.1
  191.1 231.6 %reduce-scatter.6.cloned.1.call-start = ((), (), s32[]{:S(2)}) async-start(), calls=%async_computation.4 | async-start | bytes 4718592 | tf_op jit(solution)/shard_map/reduce_scatter | solution.py:58
  306.5 202.8 %reduce-scatter.8.cloned.1.call-start = ((), (), s32[]{:S(2)}) async-start(), calls=%async_computation.5 | async-start | bytes 4718592 | tf_op jit(solution)/shard_map/reduce_scatter | solution.py:58
Sparse Core Ops, SparseCore 0:
  9.8 57.9 all-gather.6
  70.2 53.1 all-gather.8
  125.9 53.1 all-gather.10
  191.2 87.9 reduce-scatter.3
  306.6 87.7 reduce-scatter.5
  421.7 87.5 reduce-scatter.7
where the time goes:
time: 521 us; the launch traced here: 518 us
  matrix products  310 us (60%)
  waiting for transfers between devices  145 us (28%)
  local copies, waits for them, and re-layouts  33 us (6%)
  other arithmetic  15.9 us (3%)
  between operations  13.6 us (3%)
    dot_general x18, matrix products, advance(): jnp.einsum('cg,gsjq->csjq', col_onehot, lower_part, preferred_element_typ...  119 us
    dot_general x18, matrix products, advance(): jnp.einsum('gr,srjp->sgjp', row_onehot, row_panel, preferred_element_type...  87 us
    reduce_scatter x3, waiting for transfers between devices, shards(): lax.psum_scatter(partial_value, 'row', scatter_dimension=1, tiled=True)  85.5 us
    all_gather x3, waiting for transfers between devices, shards(): lax.all_gather(own_blocks[set_index:set_index + 1], 'col', axis=1, tiled=...  57.7 us
    dot_general x18, matrix products, advance(): jnp.einsum('sgjp,gpq->gsjq', picked, group_tiles, preferred_element_type=...  52 us
    dot_general x18, matrix products, advance(): jnp.einsum('cg,gsjq->csjq', col_onehot, upper_part, preferred_element_typ...  51.9 us
    while x3, local copies, waits for them, and re-layouts, live_products(): lax.fori_loop(0, turn_count, advance, jnp.zeros(acc_shape, jnp.float32))  19.7 us
    lt x18, other arithmetic, advance(): alive_mask = offset + lax.iota(jnp.int32, group_size) < live_count  11.7 us
  transfers between devices with their start and end apart: 6, of which 2 were waited for; matrix products, arithmetic and copies ran while one was open for 68% of the time, Pallas kernels for 0%

commit v1 on v0

v1 whole, which is shorter than its diff:
```python
import functools

import jax
import jax.numpy as jnp
from jax import lax
from jax.experimental import pallas as pl
from jax.experimental.pallas import tpu as pltpu
from jax.sharding import PartitionSpec as P

MESH = pl.DeviceIdType.MESH
PARTS = 1
UNROLL = 32
BF16 = jnp.bfloat16
F32 = jnp.float32


def kernel(sets, row_ref, link_ref, grad_ref, tile_ref, out_ref, *scratch):
    units = sets * PARTS
    panels = scratch[:units]
    tiles, sums, partial, got_opp, got_far, got_pair, result, send_sem, recv_sem, own_sem, tile_sem, out_sem = scratch[units:]
    slots = tiles.shape[0]
    part = panels[0].shape[1]
    own_blocks = grad_ref.shape[2]

    row = lax.axis_index("row")
    col = lax.axis_index("col")
    x, y_lo = row // 2, row % 2
    y_hi, z, core = col // 8, (col // 2) % 4, col % 2

    def col_at(yh, zz, cc):
        return (yh * 4 + (zz + 4) % 4) * 2 + cc

    def row_at(xx, yl):
        return ((xx + 4) % 4) * 2 + yl

    z_up, z_down = (row, col_at(y_hi, z + 1, core)), (row, col_at(y_hi, z - 1, core))
    y_far, sibling = (row, col_at(1 - y_hi, z, core)), (row, col_at(y_hi, z, 1 - core))
    x_up, x_down = (row_at(x + 1, y_lo), col), (row_at(x - 1, y_lo), col)
    y_pair = (row_at(x, 1 - y_lo), col)

    barrier = pltpu.get_barrier_semaphore()
    for peer in (z_up, z_down, y_far, sibling, x_up, x_down, y_pair):
        pl.semaphore_signal(barrier, inc=1, device_id=peer, device_id_type=MESH)
    pl.semaphore_wait(barrier, 7)

    def remote(u, k, src, dst, peer):
        return pltpu.make_async_remote_copy(
            src_ref=src,
            dst_ref=dst,
            send_sem=send_sem.at[u, k],
            recv_sem=recv_sem.at[u, k],
            device_id=peer,
            device_id_type=MESH,
        )

    def own_slice(u):
        s, h = u // PARTS, u % PARTS
        return grad_ref.at[s, 0, :, pl.ds(h * part, part), :]

    def shard(u, yh, zz, first=0, count=own_blocks):
        return panels[u].at[pl.ds(col_at(yh, zz, core) * own_blocks + first, count)]

    half = own_blocks // 2
    other = 1 - y_hi

    def gather_copy(u, k):
        own = shard(u, y_hi, z)
        if k < 4:
            return remote(u, k, own_slice(u), own, (z_up, z_down, y_far, sibling)[k])
        src, peer = {
            4: (shard(u, other, z), z_up),
            5: (shard(u, other, z), z_down),
            6: (shard(u, y_hi, z - 1, 0, half), z_up),
            7: (shard(u, y_hi, z + 1, half, half), z_down),
            8: (shard(u, other, z - 1, 0, half), z_up),
            9: (shard(u, other, z + 1, half, half), z_down),
            10: (shard(u, other, z), sibling),
            11: (shard(u, y_hi, z - 1), sibling),
            12: (shard(u, y_hi, z + 1), sibling),
            13: (shard(u, other, z - 1), sibling),
            14: (shard(u, other, z + 1), sibling),
            15: (shard(u, y_hi, z + 2), sibling),
            16: (shard(u, other, z + 2), sibling),
        }[k]
        return remote(u, k, src, src, peer)

    def own_copy(u):
        return pltpu.make_async_copy(own_slice(u), shard(u, y_hi, z), own_sem.at[u])

    def send(u, *ks):
        for k in ks:
            gather_copy(u, k).start()

    def arrive(u, *ks):
        for k in ks:
            gather_copy(u, k).wait_recv()

    def own_y(u):
        send(u, 2)

    def own_z(u):
        send(u, 0, 1, 3)
        own_copy(u).start()

    def ring_own(u):
        arrive(u, 0)
        send(u, 6, 11)
        arrive(u, 1)
        send(u, 7, 12)

    def ring_other(u):
        arrive(u, 2)
        send(u, 4, 5, 10)

    def ring_other_half(u):
        arrive(u, 4)
        send(u, 8, 13)
        arrive(u, 5)
        send(u, 9, 14)

    def opposite_own(u):
        arrive(u, 6, 7)
        send(u, 15)

    def opposite_other(u):
        arrive(u, 8, 9)
        send(u, 16)

    def gathered(u):
        own_copy(u).wait()
        arrive(u, 3, 10, 11, 12, 13, 14, 15, 16)

    def products(u, first, count):
        def some(step, carry):
            for k in range(UNROLL):
                t = first + step * UNROLL + k
                picked = panels[u][row_ref[t]]
                sums[t] = sums[link_ref[t]] + jnp.dot(picked, tiles[t], preferred_element_type=F32)
            return carry

        lax.fori_loop(0, count // UNROLL, some, 0)

    def share(u, xx, yl):
        return partial.at[u, pl.ds(row_at(xx, yl) * own_blocks, own_blocks)]

    def collect(u, xx):
        first = row_at(xx, 0) * own_blocks

        def some(step, carry):
            for k in range(4):
                i = first + step * 4 + k
                partial[u, i] = sums[link_ref[slots + i]].astype(BF16)
            return carry

        lax.fori_loop(0, 2 * own_blocks // 4, some, 0)

    def reduce_copy(u, k):
        src, dst, peer = {
            17: (share(u, x + 2, 0), got_opp.at[u, 0], x_up),
            18: (share(u, x + 2, 1), got_opp.at[u, 1], x_down),
            19: (share(u, x + 1, 1), got_far.at[u, 0, 1], x_up),
            20: (share(u, x - 1, 0), got_far.at[u, 1, 0], x_down),
            21: (share(u, x + 1, 0), got_far.at[u, 0, 0], x_up),
            22: (share(u, x - 1, 1), got_far.at[u, 1, 1], x_down),
            23: (share(u, x, 1 - y_lo), got_pair.at[u], y_pair),
        }[k]
        return remote(u, k, src, dst, peer)

    def reduce_first(u):
        collect(u, x + 2)
        reduce_copy(u, 17).start()
        reduce_copy(u, 18).start()
        collect(u, x + 1)
        reduce_copy(u, 19).start()
        collect(u, x - 1)
        reduce_copy(u, 20).start()
        collect(u, x)

    def add_share(u, xx, yl, terms):
        first = row_at(xx, yl) * own_blocks

        def some(i, carry):
            total = partial[u, first + i].astype(F32)
            for term in terms:
                total = total + term(i).astype(F32)
            partial[u, first + i] = total.astype(BF16)
            return carry

        lax.fori_loop(0, own_blocks, some, 0)

    def reduce_second(u):
        reduce_copy(u, 17).wait_recv()
        add_share(u, x + 1, 0, [lambda i: got_opp[u, 0, i]])
        reduce_copy(u, 21).start()
        reduce_copy(u, 18).wait_recv()
        add_share(u, x - 1, 1, [lambda i: got_opp[u, 1, i]])
        reduce_copy(u, 22).start()

    def reduce_third(u):
        for k in (19, 20, 21, 22):
            reduce_copy(u, k).wait_recv()
        theirs = 1 - y_lo
        add_share(u, x, theirs, [lambda i: got_far[u, 0, theirs, i], lambda i: got_far[u, 1, theirs, i]])
        reduce_copy(u, 23).start()

    def out_copy(u):
        s, h = u // PARTS, u % PARTS
        return pltpu.make_async_copy(result.at[u], out_ref.at[s, 0, :, pl.ds(h * part, part), :], out_sem.at[u])

    def reduce_last(u):
        reduce_copy(u, 23).wait_recv()
        first = row_at(x, y_lo) * own_blocks

        def some(i, carry):
            total = partial[u, first + i].astype(F32) + got_far[u, 0, y_lo, i].astype(F32)
            total = total + got_far[u, 1, y_lo, i].astype(F32)
            result[u, i] = (total + got_pair[u, i].astype(F32)).astype(BF16)
            return carry

        lax.fori_loop(0, own_blocks, some, 0)
        out_copy(u).start()

    run = slots // 4
    tile_copies = [
        pltpu.make_async_copy(tile_ref.at[pl.ds(q * run, run)], tiles.at[pl.ds(q * run, run)], tile_sem.at[q])
        for q in range(4)
    ]
    own_y(0)
    own_z(0)
    for copy in tile_copies:
        copy.start()
    sums[slots] = jnp.zeros(sums.shape[1:], F32)

    def on(action, u):
        if 0 <= u < units:
            action(u)

    ring_own(0)
    on(own_z, 1)
    ring_other(0)
    on(own_y, 1)
    ring_other_half(0)
    opposite_own(0)
    opposite_other(0)
    gathered(0)
    for copy in tile_copies:
        copy.wait()
    for u in range(units):
        products(u, 0, run)
        on(ring_own, u + 1)
        on(own_z, u + 2)
        products(u, run, run)
        on(ring_other, u + 1)
        on(own_y, u + 2)
        products(u, 2 * run, run)
        on(reduce_third, u - 1)
        products(u, 3 * run, run)
        reduce_first(u)
        on(ring_other_half, u + 1)
        on(opposite_own, u + 1)
        on(reduce_second, u)
        on(reduce_last, u - 1)
        on(opposite_other, u + 1)
        on(gathered, u + 1)
    reduce_third(units - 1)
    reduce_last(units - 1)
    for u in range(units):
        for k in range(17):
            gather_copy(u, k).wait_send()
        for k in range(17, 24):
            reduce_copy(u, k).wait_send()
        out_copy(u).wait()


def shards(gradients, tile_blocks, tile_rows, tile_cols, tile_counts):
    sets, _, own_blocks, objectives, pores = gradients.shape
    slots = tile_blocks.shape[0]
    row_blocks = own_blocks * lax.axis_size("col")
    column_blocks = own_blocks * lax.axis_size("row")
    units, part = sets * PARTS, objectives // PARTS

    order = lax.iota(jnp.int32, slots)
    wanted = jnp.concatenate([tile_cols, lax.iota(jnp.int32, column_blocks)])
    limit = jnp.concatenate([order, jnp.broadcast_to(tile_counts, (column_blocks,))])
    match = (tile_cols[None, :] == wanted[:, None]) & (order[None, :] < limit[:, None])
    found = jnp.max(jnp.where(match, order[None, :], -1), axis=1)
    link = jnp.where(found < 0, slots, found)

    any_space = pl.BlockSpec(memory_space=pl.ANY)
    smem = pl.BlockSpec(memory_space=pltpu.SMEM)
    return pl.pallas_call(
        functools.partial(kernel, sets),
        out_shape=jax.ShapeDtypeStruct(gradients.shape, BF16),
        in_specs=[smem, smem, any_space, any_space],
        out_specs=any_space,
        scratch_shapes=[pltpu.VMEM((row_blocks, part, pores), BF16) for _ in range(units)]
        + [
            pltpu.VMEM((slots, pores, pores), BF16),
            pltpu.VMEM((slots + 1, part, pores), F32),
            pltpu.VMEM((units, column_blocks, part, pores), BF16),
            pltpu.VMEM((units, 2, own_blocks, part, pores), BF16),
            pltpu.VMEM((units, 2, 2, own_blocks, part, pores), BF16),
            pltpu.VMEM((units, own_blocks, part, pores), BF16),
            pltpu.VMEM((units, own_blocks, part, pores), BF16),
            pltpu.SemaphoreType.DMA((units, 24)),
            pltpu.SemaphoreType.DMA((units, 24)),
            pltpu.SemaphoreType.DMA((units,)),
            pltpu.SemaphoreType.DMA((4,)),
            pltpu.SemaphoreType.DMA((units,)),
        ],
        compiler_params=pltpu.CompilerParams(
            collective_id=0, has_side_effects=True, vmem_limit_bytes=60 * 2**20
        ),
        cost_estimate=pl.CostEstimate(
            flops=2 * sets * slots * objectives * pores * pores, bytes_accessed=slots * pores * pores * 2, transcendentals=0
        ),
    )(tile_rows, link, gradients, tile_blocks)


def solution(mesh):
    in_specs = (
        P(None, "row", "col", None, None),
        P(("row", "col"), None, None),
        P(("row", "col")),
        P(("row", "col")),
        P(("row", "col")),
    )
    out_specs = P(None, "col", "row", None, None)
    return jax.shard_map(shards, mesh=mesh, in_specs=in_specs, out_specs=out_specs, check_vma=False)
```

time: 521 us -> 119 us (0.23)
  matrix products: 310 us -> 0 us
  waiting for transfers between devices: 145 us -> 0 us
  Pallas kernels: 0 us -> 113 us
  local copies, waits for them, and re-layouts: 33 us -> 2.07 us
  other arithmetic: 15.9 us -> 2.26 us
  between operations: 13.6 us -> 0.67 us
    dot_general x72 -> x0, matrix products: 310 us -> none  [the longest x18 119 us: advance(): jnp.einsum('cg,gsjq->csjq', col_onehot, lower_part, preferred_element_typ...]
    pallas_call x0 -> x1, Pallas kernels: none -> 113 us  [shards(): pl.pallas_call(functools.partial(kernel, sets), out_shape=jax.ShapeDtypeS...]
    reduce_scatter x3 -> x0, waiting for transfers between devices: 85.5 us -> none  [shards(): lax.psum_scatter(partial_value, 'row', scatter_dimension=1, tiled=True)]
    all_gather x3 -> x0, waiting for transfers between devices: 57.7 us -> none  [shards(): lax.all_gather(own_blocks[set_index:set_index + 1], 'col', axis=1, tiled=...]
    while x3 -> x0, local copies, waits for them, and re-layouts: 19.7 us -> none  [live_products(): lax.fori_loop(0, turn_count, advance, jnp.zeros(acc_shape, jnp.float32))]
    lt x18 -> x0, other arithmetic: 11.7 us -> none  [advance(): alive_mask = offset + lax.iota(jnp.int32, group_size) < live_count]
    dynamic_slice x36 -> x0, local copies, waits for them, and re-layouts: 10.8 us -> none  [the longest x18 5.44 us: advance(): group_cols = lax.dynamic_slice_in_dim(col_ids, offset, group_size, 0)]
  transfers between devices with their start and end apart: 6 -> 0, of which waited for: 2 -> 0; matrix products, arithmetic and copies ran while one was open for 68% -> 0% of each run, Pallas kernels for 0% -> 0%
where the time goes in v1:
time: 119 us; the launch traced here: 118 us
  Pallas kernels  113 us (95%)
  other arithmetic  2.26 us (2%)
  local copies, waits for them, and re-layouts  2.07 us (2%)
    pallas_call x1, Pallas kernels, shards(): pl.pallas_call(functools.partial(kernel, sets), out_shape=jax.ShapeDtypeS...  113 us

profile of v1, /device:TPU:0, one launch (start us, length us, event | category | flops | bytes accessed | tf_op | source)
XLA Modules:
  0.0 118.5 jit_solution(15027951143107585263)
XLA Ops:
  0.7 0.7 pad_add_fusion
  1.4 1.0 select_reduce_fusion
  2.3 0.6 compare_select_fusion.link_ref
  2.9 113.5 %shard_map.55 = bf16[3,1,16,64,128]{4,3,2,1,0:T(8,128)(2,1)} custom-call(s32[384]{0:T(512)} %row_ref.1, s32[512]{0:T(512)} %compare_select_fusion.link_ref, bf16[3,1,16,64,128]{4,3,2,1,0:T(8,128)(2,1)} %grad_ref.1, bf16[384,128,128]{2,1,0:T(8,128)(2,1)} %tile_ref.1), custom_call_target="tpu_custom_call" | custom-call | flops 2415919104 | bytes 12582912 | tf_op jit(solution)/shard_map/pallas_call | solution.py:291
  116.4 2.1 %copy.8 = bf16[3,1,16,64,128]{4,3,2,1,0:T(8,128)(2,1)} copy(bf16[3,1,16,64,128]{4,3,2,1,0:T(8,128)(2,1)} %shard_map.55) | data formatting | bytes 1572864
  (3 shorter events, 0.0 us)

commit v2 on v1

--- a/solution.py
+++ b/solution.py
@@ -8,16 +8,38 @@
 from jax.sharding import PartitionSpec as P
 
 MESH = pl.DeviceIdType.MESH
-PARTS = 1
+PARTS = 2
+SIDE = 4
+ORDER = (
+    ("own_z", 0), ("own_z", 2), ("own_z", 1), ("own_y", 3), ("own_y", 0), ("ring_other", 0), ("own_y", 1),
+    ("ring_own_a", 0), ("ring_own_b", 0), ("own_y", 2), ("ring_other", 1), ("opposite_own", 0), ("half_b", 0),
+    ("half_a", 0), ("own_y", 4), ("ring_own_b", 1), ("ring_own_a", 1), ("opposite_other", 0), ("own_z", 3),
+    ("ring_other", 2), ("half_a", 1), ("half_b", 1), ("ring_own_a", 2), ("ring_own_b", 2), ("opposite_own", 1),
+    ("gathered", 0), ("p0", 0), ("own_y", 5), ("p1", 0), ("p2", 0), ("opposite_other", 1), ("p3", 0),
+    ("reduce_first", 0), ("gathered", 1), ("p0", 1), ("ring_other", 3), ("opposite_own", 2), ("p1", 1),
+    ("half_a", 2), ("half_b", 2), ("p2", 1), ("p3", 1), ("reduce_first", 1), ("opposite_other", 2),
+    ("ring_own_b", 3), ("own_z", 4), ("ring_own_a", 3), ("second_b", 0), ("gathered", 2), ("p0", 2), ("half_b", 3),
+    ("second_a", 0), ("half_a", 3), ("p1", 2), ("ring_other", 4), ("opposite_own", 3), ("own_z", 5), ("p2", 2),
+    ("p3", 2), ("opposite_other", 3), ("ring_other", 5), ("reduce_first", 2), ("gathered", 3), ("reduce_third", 0),
+    ("p0", 3), ("ring_own_a", 4), ("second_a", 1), ("p1", 3), ("ring_own_b", 4), ("second_b", 1), ("p2", 3),
+    ("p3", 3), ("ring_own_a", 5), ("half_b", 5), ("half_b", 4), ("opposite_own", 4), ("reduce_first", 3),
+    ("half_a", 5), ("ring_own_b", 5), ("half_a", 4), ("opposite_other", 4), ("opposite_own", 5), ("gathered", 4),
+    ("second_b", 2), ("second_a", 2), ("p0", 4), ("opposite_other", 5), ("p1", 4), ("second_a", 3), ("gathered", 5),
+    ("second_b", 3), ("p2", 4), ("p3", 4), ("reduce_first", 4), ("reduce_third", 2), ("p0", 5), ("p1", 5),
+    ("reduce_third", 3), ("p2", 5), ("p3", 5), ("reduce_first", 5), ("reduce_last", 2), ("reduce_last", 3),
+    ("second_b", 4), ("reduce_third", 1), ("second_a", 4), ("second_a", 5), ("second_b", 5), ("reduce_third", 4),
+    ("reduce_third", 5), ("reduce_last", 0), ("reduce_last", 1), ("reduce_last", 4), ("reduce_last", 5),
+)
 UNROLL = 32
+LANES = 128
 BF16 = jnp.bfloat16
 F32 = jnp.float32
 
 
-def kernel(sets, row_ref, link_ref, grad_ref, tile_ref, out_ref, *scratch):
+def kernel(sets, row_ref, col_ref, count_ref, cols_ref, grad_ref, tile_ref, out_ref, *scratch):
     units = sets * PARTS
     panels = scratch[:units]
-    tiles, sums, partial, got_opp, got_far, got_pair, result, send_sem, recv_sem, own_sem, tile_sem, out_sem = scratch[units:]
+    tiles, sums, partial, got_opp, got_far, got_pair, result, wanted, found, link_ref, send_sem, recv_sem, own_sem, tile_sem, out_sem, link_sem = scratch[units:]
     slots = tiles.shape[0]
     part = panels[0].shape[1]
     own_blocks = grad_ref.shape[2]
@@ -72,8 +94,9 @@
             5: (shard(u, other, z), z_down),
             6: (shard(u, y_hi, z - 1, 0, half), z_up),
             7: (shard(u, y_hi, z + 1, half, half), z_down),
-            8: (shard(u, other, z - 1, 0, half), z_up),
-            9: (shard(u, other, z + 1, half, half), z_down),
+            8: (shard(u, other, z - 1, 0, SIDE), z_up),
+            9: (shard(u, other, z + 1, own_blocks - SIDE, SIDE), z_down),
+            24: (shard(u, y_hi, z + 2, SIDE, own_blocks - 2 * SIDE), y_far),
             10: (shard(u, other, z), sibling),
             11: (shard(u, y_hi, z - 1), sibling),
             12: (shard(u, y_hi, z + 1), sibling),
@@ -102,9 +125,11 @@
         send(u, 0, 1, 3)
         own_copy(u).start()
 
-    def ring_own(u):
+    def ring_own_a(u):
         arrive(u, 0)
         send(u, 6, 11)
+
+    def ring_own_b(u):
         arrive(u, 1)
         send(u, 7, 12)
 
@@ -112,23 +137,55 @@
         arrive(u, 2)
         send(u, 4, 5, 10)
 
-    def ring_other_half(u):
+    def half_a(u):
         arrive(u, 4)
         send(u, 8, 13)
+
+    def half_b(u):
         arrive(u, 5)
         send(u, 9, 14)
 
     def opposite_own(u):
         arrive(u, 6, 7)
-        send(u, 15)
+        send(u, 24, 15)
 
     def opposite_other(u):
-        arrive(u, 8, 9)
+        arrive(u, 8, 9, 24)
         send(u, 16)
 
     def gathered(u):
         own_copy(u).wait()
         arrive(u, 3, 10, 11, 12, 13, 14, 15, 16)
+
+    def cols_copy(i):
+        return pltpu.make_async_copy(cols_ref.at[pl.ds(i * LANES, LANES)], wanted.at[i], link_sem.at[i])
+
+    def link_copy(i):
+        return pltpu.make_async_copy(found.at[i], link_ref.at[pl.ds(i * LANES, LANES)], link_sem.at[i])
+
+    def link_start():
+        wanted[...] = jnp.zeros(wanted.shape, jnp.int32)
+        for i in range(slots // LANES):
+            cols_copy(i).start()
+
+    def link_slots():
+        for i in range(slots // LANES):
+            cols_copy(i).wait()
+        at = lax.broadcasted_iota(jnp.int32, wanted.shape, 0) * LANES + lax.broadcasted_iota(jnp.int32, wanted.shape, 1)
+        target = jnp.where(at < slots, wanted[...], at - slots)
+        limit = jnp.where(at < slots, at, count_ref[0])
+
+        def some(step, latest):
+            for k in range(16):
+                t = step * 16 + k
+                latest = jnp.where((target == col_ref[t]) & (limit > t), t, latest)
+            return latest
+
+        found[...] = lax.fori_loop(0, slots // 16, some, jnp.full(wanted.shape, slots, jnp.int32))
+        for i in range(wanted.shape[0]):
+            link_copy(i).start()
+        for i in range(wanted.shape[0]):
+            link_copy(i).wait()
 
     def products(u, first, count):
         def some(step, carry):
@@ -188,10 +245,12 @@
 
         lax.fori_loop(0, own_blocks, some, 0)
 
-    def reduce_second(u):
+    def second_a(u):
         reduce_copy(u, 17).wait_recv()
         add_share(u, x + 1, 0, [lambda i: got_opp[u, 0, i]])
         reduce_copy(u, 21).start()
+
+    def second_b(u):
         reduce_copy(u, 18).wait_recv()
         add_share(u, x - 1, 1, [lambda i: got_opp[u, 1, i]])
         reduce_copy(u, 22).start()
@@ -225,47 +284,35 @@
         pltpu.make_async_copy(tile_ref.at[pl.ds(q * run, run)], tiles.at[pl.ds(q * run, run)], tile_sem.at[q])
         for q in range(4)
     ]
-    own_y(0)
-    own_z(0)
-    for copy in tile_copies:
-        copy.start()
-    sums[slots] = jnp.zeros(sums.shape[1:], F32)
-
-    def on(action, u):
-        if 0 <= u < units:
-            action(u)
-
-    ring_own(0)
-    on(own_z, 1)
-    ring_other(0)
-    on(own_y, 1)
-    ring_other_half(0)
-    opposite_own(0)
-    opposite_other(0)
-    gathered(0)
-    for copy in tile_copies:
-        copy.wait()
+
+    def product_run(q):
+        def action(u):
+            if u == 0:
+                if q == 0:
+                    link_slots()
+                tile_copies[q].wait()
+            products(u, q * run, run)
+
+        return action
+
+    actions = {f"p{q}": product_run(q) for q in range(4)}
+    for action in (
+        own_y, own_z, ring_own_a, ring_own_b, ring_other, half_a, half_b, opposite_own, opposite_other, gathered,
+        reduce_first, second_a, second_b, reduce_third, reduce_last,
+    ):
+        actions[action.__name__] = action
+
+    started = False
+    for name, u in ORDER:
+        if not started and name.startswith("ring"):
+            started = True
+            link_start()
+            for copy in tile_copies:
+                copy.start()
+            sums[slots] = jnp.zeros(sums.shape[1:], F32)
+        actions[name](u)
     for u in range(units):
-        products(u, 0, run)
-        on(ring_own, u + 1)
-        on(own_z, u + 2)
-        products(u, run, run)
-        on(ring_other, u + 1)
-        on(own_y, u + 2)
-        products(u, 2 * run, run)
-        on(reduce_third, u - 1)
-        products(u, 3 * run, run)
-        reduce_first(u)
-        on(ring_other_half, u + 1)
-        on(opposite_own, u + 1)
-        on(reduce_second, u)
-        on(reduce_last, u - 1)
-        on(opposite_other, u + 1)
-        on(gathered, u + 1)
-    reduce_third(units - 1)
-    reduce_last(units - 1)
-    for u in range(units):
-        for k in range(17):
+        for k in (*range(17), 24):
             gather_copy(u, k).wait_send()
         for k in range(17, 24):
             reduce_copy(u, k).wait_send()
@@ -279,19 +326,12 @@
     column_blocks = own_blocks * lax.axis_size("row")
     units, part = sets * PARTS, objectives // PARTS
 
-    order = lax.iota(jnp.int32, slots)
-    wanted = jnp.concatenate([tile_cols, lax.iota(jnp.int32, column_blocks)])
-    limit = jnp.concatenate([order, jnp.broadcast_to(tile_counts, (column_blocks,))])
-    match = (tile_cols[None, :] == wanted[:, None]) & (order[None, :] < limit[:, None])
-    found = jnp.max(jnp.where(match, order[None, :], -1), axis=1)
-    link = jnp.where(found < 0, slots, found)
-
     any_space = pl.BlockSpec(memory_space=pl.ANY)
     smem = pl.BlockSpec(memory_space=pltpu.SMEM)
     return pl.pallas_call(
         functools.partial(kernel, sets),
         out_shape=jax.ShapeDtypeStruct(gradients.shape, BF16),
-        in_specs=[smem, smem, any_space, any_space],
+        in_specs=[smem, smem, smem, any_space, any_space, any_space],
         out_specs=any_space,
         scratch_shapes=[pltpu.VMEM((row_blocks, part, pores), BF16) for _ in range(units)]
         + [
@@ -302,11 +342,15 @@
             pltpu.VMEM((units, 2, 2, own_blocks, part, pores), BF16),
             pltpu.VMEM((units, own_blocks, part, pores), BF16),
             pltpu.VMEM((units, own_blocks, part, pores), BF16),
-            pltpu.SemaphoreType.DMA((units, 24)),
-            pltpu.SemaphoreType.DMA((units, 24)),
+            pltpu.VMEM(((slots + column_blocks) // LANES, LANES), jnp.int32),
+            pltpu.VMEM(((slots + column_blocks) // LANES, LANES), jnp.int32),
+            pltpu.SMEM((slots + column_blocks,), jnp.int32),
+            pltpu.SemaphoreType.DMA((units, 25)),
+            pltpu.SemaphoreType.DMA((units, 25)),
             pltpu.SemaphoreType.DMA((units,)),
             pltpu.SemaphoreType.DMA((4,)),
             pltpu.SemaphoreType.DMA((units,)),
+            pltpu.SemaphoreType.DMA(((slots + column_blocks) // LANES,)),
         ],
         compiler_params=pltpu.CompilerParams(
             collective_id=0, has_side_effects=True, vmem_limit_bytes=60 * 2**20
@@ -314,7 +358,7 @@
         cost_estimate=pl.CostEstimate(
             flops=2 * sets * slots * objectives * pores * pores, bytes_accessed=slots * pores * pores * 2, transcendentals=0
         ),
-    )(tile_rows, link, gradients, tile_blocks)
+    )(tile_rows, tile_cols, tile_counts, tile_cols, gradients, tile_blocks)
 
 
 def solution(mesh):

time: 119 us -> 104 us (0.87)
  Pallas kernels: 113 us -> 101 us
  other arithmetic: 2.26 us -> 0 us
    pallas_call x1, Pallas kernels: 113 us -> 101 us  [shards(): pl.pallas_call(functools.partial(kernel, sets), out_shape=jax.ShapeDtypeS...]
where the time goes in v2:
time: 104 us; the launch traced here: 103 us
  Pallas kernels  101 us (97%)
  local copies, waits for them, and re-layouts  2.06 us (2%)
    pallas_call x1, Pallas kernels, shards(): pl.pallas_call(functools.partial(kernel, sets), out_shape=jax.ShapeDtypeS...  101 us

profile of v2, /device:TPU:0, one launch (start us, length us, event | category | flops | bytes accessed | tf_op | source)
XLA Modules:
  0.0 103.4 jit_solution(1346603809440227826)
XLA Ops:
  0.7 100.6 %shard_map.55 = bf16[3,1,16,64,128]{4,3,2,1,0:T(8,128)(2,1)} custom-call(s32[384]{0:T(512)} %row_ref.1, s32[384]{0:T(512)} %cols_ref.1, s32[1]{0:T(128)S(6)} %copy.7.count_ref, s32[384]{0:T(512)} %cols_ref.1, bf16[3,1,16,64,128]{4,3,2,1,0:T(8,128)(2,1)} %grad_ref.1, bf16[384,128,128]{2,1,0:T(8,128)(2,1)} %tile_ref.1), custom_call_target="tpu_custom_call" | custom-call | flops 2415919104 | bytes 12582912 | tf_op jit(solution)/shard_map/pallas_call | solution.py:331
  101.3 2.1 %copy.8 = bf16[3,1,16,64,128]{4,3,2,1,0:T(8,128)(2,1)} copy(bf16[3,1,16,64,128]{4,3,2,1,0:T(8,128)(2,1)} %shard_map.55) | data formatting | bytes 1572864

commit v3 on v2

v3 whole, which is shorter than its diff:
```python
import functools

import jax
import jax.numpy as jnp
from jax import lax
from jax.experimental import pallas as pl
from jax.experimental.pallas import tpu as pltpu
from jax.sharding import PartitionSpec as P

MESH = pl.DeviceIdType.MESH
PARTS = 2
SIDE = (4, 4, 4, 4, 4, 4)
PAIRED = (False, False, True, True, True, True)
ORDER = (
    ("own_z", 1), ("own_y", 1), ("own_z", 2), ("ring_other", 1), ("own_y", 0), ("own_y", 2), ("ring_own_b", 1),
    ("ring_own_a", 1), ("ring_own_b", 2), ("ring_own_a", 2), ("ring_other", 2), ("half_b", 1), ("half_a", 1),
    ("opposite_own", 1), ("opposite_other", 1), ("own_z", 0), ("own_y", 4), ("opposite_own", 2), ("own_y", 3),
    ("half_a", 2), ("half_b", 2), ("gathered", 1), ("p0", 1), ("ring_other", 0), ("p1", 1), ("p2", 1), ("own_z", 3),
    ("own_y", 5), ("ring_own_a", 0), ("ring_own_b", 0), ("opposite_other", 2), ("p3", 1), ("reduce_first", 1),
    ("gathered", 2), ("p0", 2), ("p1", 2), ("half_b", 0), ("half_a", 0), ("opposite_own", 0), ("ring_other", 3),
    ("p2", 2), ("ring_own_a", 3), ("p3", 2), ("opposite_other", 0), ("ring_own_b", 3), ("reduce_first", 2),
    ("own_z", 4), ("second_a", 1), ("second_b", 1), ("gathered", 0), ("p0", 0), ("half_b", 3), ("p1", 0),
    ("opposite_own", 3), ("half_a", 3), ("ring_other", 4), ("side", 2), ("p2", 0), ("p3", 0), ("opposite_other", 3),
    ("ring_own_b", 4), ("ring_own_a", 4), ("reduce_first", 0), ("own_z", 5), ("reduce_third", 1), ("gathered", 3),
    ("p0", 3), ("second_b", 2), ("p1", 3), ("half_a", 4), ("opposite_own", 4), ("half_b", 4), ("second_a", 2),
    ("ring_other", 5), ("p2", 3), ("p3", 3), ("opposite_other", 4), ("ring_own_a", 5), ("ring_own_b", 5),
    ("reduce_first", 3), ("second_b", 0), ("second_a", 0), ("gathered", 4), ("p0", 4), ("half_b", 5), ("half_a", 5),
    ("opposite_own", 5), ("p1", 4), ("p2", 4), ("side", 3), ("opposite_other", 5), ("p3", 4), ("reduce_first", 4),
    ("gathered", 5), ("p0", 5), ("reduce_third", 2), ("second_b", 3), ("second_a", 3), ("p1", 5), ("p2", 5),
    ("side", 4), ("p3", 5), ("reduce_first", 5), ("second_a", 4), ("reduce_third", 3), ("second_b", 4),
    ("reduce_third", 0), ("side", 5), ("second_b", 5), ("second_a", 5), ("reduce_third", 4), ("reduce_last", 0),
    ("reduce_last", 1), ("reduce_last", 2), ("reduce_third", 5), ("reduce_last", 4), ("reduce_last", 3),
    ("reduce_last", 5),
)
UNROLL = 32
LANES = 128
RECV = (0, 1, 2, 3, 4, 5, 6, 6, 7, 7, 3, 3, 3, 3, 3, 3, 3, 8, 9, 10, 10, 10, 10, 11, 7, 12)
ARRIVALS = 13
BF16 = jnp.bfloat16
F32 = jnp.float32


def kernel(sets, count_ref, rows_ref, cols_ref, grad_ref, tile_ref, out_ref, *scratch):
    units = sets * PARTS
    panels = scratch[:units]
    (
        tiles, sums, partial, got_opp, got_far, got_pair, got_side, result, wanted, found, link_ref, col_ref,
        send_sem, recv_sem, own_sem, tile_sem, out_sem, link_sem,
    ) = scratch[units:]
    slots = tiles.shape[0]
    part, pores = panels[0].shape[1:]
    own_blocks = grad_ref.shape[2]

    row = lax.axis_index("row")
    col = lax.axis_index("col")
    x, y_lo = row // 2, row % 2
    y_hi, z, core = col // 8, (col // 2) % 4, col % 2

    def col_at(yh, zz, cc):
        return (yh * 4 + (zz + 4) % 4) * 2 + cc

    def row_at(xx, yl):
        return ((xx + 4) % 4) * 2 + yl

    z_up, z_down = (row, col_at(y_hi, z + 1, core)), (row, col_at(y_hi, z - 1, core))
    y_far, sibling = (row, col_at(1 - y_hi, z, core)), (row, col_at(y_hi, z, 1 - core))
    x_up, x_down = (row_at(x + 1, y_lo), col), (row_at(x - 1, y_lo), col)
    y_pair = (row_at(x, 1 - y_lo), col)

    barrier = pltpu.get_barrier_semaphore()
    for peer in (z_up, z_down, y_far, sibling, x_up, x_down, y_pair):
        pl.semaphore_signal(barrier, inc=1, device_id=peer, device_id_type=MESH)
    pl.semaphore_wait(barrier, 7)

    def remote(u, k, src, dst, peer):
        return pltpu.make_async_remote_copy(
            src_ref=src,
            dst_ref=dst,
            send_sem=send_sem.at[u],
            recv_sem=recv_sem.at[u, RECV[k]],
            device_id=peer,
            device_id_type=MESH,
        )

    def landed(u, k, region):
        remote(u, k, region, region, sibling).wait_recv()

    def own_slice(u):
        s, h = u // PARTS, u % PARTS
        return grad_ref.at[s, 0, :, pl.ds(h * part, part), :]

    def shard(u, yh, zz, first=0, count=own_blocks):
        return panels[u].at[pl.ds((core * 8 + yh * 4 + (zz + 4) % 4) * own_blocks + first, count)]

    half = own_blocks // 2
    other = 1 - y_hi

    def gather_copy(u, k):
        own = shard(u, y_hi, z)
        if k < 4:
            return remote(u, k, own_slice(u), own, (z_up, z_down, y_far, sibling)[k])
        src, peer = {
            4: (shard(u, other, z), z_up),
            5: (shard(u, other, z), z_down),
            6: (shard(u, y_hi, z - 1, 0, half), z_up),
            7: (shard(u, y_hi, z + 1, half, half), z_down),
            8: (shard(u, other, z - 1, 0, SIDE[u]), z_up),
            9: (shard(u, other, z + 1, own_blocks - SIDE[u], SIDE[u]), z_down),
            24: (shard(u, y_hi, z + 2, SIDE[u], own_blocks - 2 * SIDE[u]), y_far),
            10: (shard(u, other, z), sibling),
            11: (shard(u, y_hi, z - 1), sibling),
            12: (shard(u, y_hi, z + 1), sibling),
            13: (shard(u, other, z - 1), sibling),
            14: (shard(u, other, z + 1), sibling),
            15: (shard(u, y_hi, z + 2), sibling),
            16: (shard(u, other, z + 2), sibling),
        }[k]
        return remote(u, k, src, src, peer)

    def own_copy(u):
        return pltpu.make_async_copy(own_slice(u), shard(u, y_hi, z), own_sem.at[u])

    def send(u, *ks):
        for k in ks:
            gather_copy(u, k).start()

    def arrive(u, *ks):
        for k in ks:
            gather_copy(u, k).wait_recv()

    def own_y(u):
        send(u, 2)

    def own_z(u):
        send(u, 0, 1, 3)
        own_copy(u).start()

    def ring_own_a(u):
        arrive(u, 0)
        send(u, 6, 11)

    def ring_own_b(u):
        arrive(u, 1)
        send(u, 7, 12)

    def ring_other(u):
        arrive(u, 2)
        send(u, 4, 5, 10)

    def half_a(u):
        arrive(u, 4)
        send(u, 8, 13)

    def half_b(u):
        arrive(u, 5)
        send(u, 9, 14)

    def opposite_own(u):
        landed(u, 6, shard(u, y_hi, z + 2))
        if SIDE[u] < half:
            send(u, 24)
        send(u, 15)

    def opposite_other(u):
        landed(u, 8, shard(u, other, z + 2))
        send(u, 16)

    def gathered(u):
        own_copy(u).wait()
        landed(u, 3, panels[u].at[pl.ds((1 - core) * 8 * own_blocks, 8 * own_blocks)])

    lines = slots // LANES
    linked = slots + partial.shape[1]
    link_lines = linked // LANES

    def index_copies():
        copies = [pltpu.make_async_copy(cols_ref, col_ref, link_sem.at[0])]
        for i in range(lines):
            run_i = pl.ds(i * LANES, LANES)
            copies.append(pltpu.make_async_copy(cols_ref.at[run_i], wanted.at[i], link_sem.at[1 + i]))
            copies.append(pltpu.make_async_copy(rows_ref.at[run_i], wanted.at[link_lines + i], link_sem.at[1 + lines + i]))
        return copies

    def link_start():
        wanted[...] = jnp.zeros(wanted.shape, jnp.int32)
        for copy in index_copies():
            copy.start()

    def link_slots():
        for copy in index_copies():
            copy.wait()
        shape = (link_lines, LANES)
        at = lax.broadcasted_iota(jnp.int32, shape, 0) * LANES + lax.broadcasted_iota(jnp.int32, shape, 1)
        target = jnp.where(at < slots, wanted[:link_lines], at - slots)
        limit = jnp.where(at < slots, at, count_ref[0])

        def some(step, latest):
            for k in range(16):
                t = step * 16 + k
                latest = jnp.where((target == col_ref[t]) & (limit > t), t, latest)
            return latest

        found[:link_lines] = lax.fori_loop(0, slots // 16, some, jnp.full(shape, slots, jnp.int32))
        rows = wanted[link_lines:]
        group = rows // own_blocks
        found[link_lines:] = ((group % 2) * 8 + group // 2) * own_blocks + rows % own_blocks
        copies = [
            pltpu.make_async_copy(found.at[i], link_ref.at[pl.ds(i * LANES, LANES)], link_sem.at[i])
            for i in range(link_lines + lines)
        ]
        for copy in copies:
            copy.start()
        for copy in copies:
            copy.wait()

    def products(u, first, count):
        def some(step, carry):
            for k in range(UNROLL):
                t = first + step * UNROLL + k
                picked = panels[u][link_ref[linked + t]]
                sums[t] = sums[link_ref[t]] + jnp.dot(picked, tiles[t], preferred_element_type=F32)
            return carry

        lax.fori_loop(0, count // UNROLL, some, 0)

    theirs = 1 - y_lo

    def share(u, xx, yl, first=0, count=own_blocks):
        return partial.at[u, pl.ds(row_at(xx, yl) * own_blocks + first, count)]

    def collect(u, xx):
        first = row_at(xx, 0) * own_blocks

        def some(step, carry):
            for k in range(4):
                i = first + step * 4 + k
                partial[u, i] = sums[link_ref[slots + i]].astype(BF16)
            return carry

        lax.fori_loop(0, 2 * own_blocks // 4, some, 0)

    def reduce_copy(u, k):
        if PAIRED[u]:
            src, dst, peer = {
                17: (share(u, x + 2, y_lo, 0, half), got_opp.at[u, 0, pl.ds(0, half)], x_up),
                18: (share(u, x + 2, y_lo, half, half), got_opp.at[u, 1, pl.ds(half, half)], x_down),
                19: (share(u, x + 1, theirs), got_far.at[u, 0, theirs], x_up),
                20: (share(u, x - 1, theirs), got_far.at[u, 1, theirs], x_down),
                21: (share(u, x + 1, y_lo), got_far.at[u, 0, y_lo], x_up),
                22: (share(u, x - 1, y_lo), got_far.at[u, 1, y_lo], x_down),
                23: (share(u, x, theirs), got_pair.at[u], y_pair),
                25: (share(u, x + 2, theirs), got_side.at[u], y_pair),
            }[k]
        else:
            src, dst, peer = {
                17: (share(u, x + 2, 0), got_opp.at[u, 0], x_up),
                18: (share(u, x + 2, 1), got_opp.at[u, 1], x_down),
                19: (share(u, x + 1, 1), got_far.at[u, 0, 1], x_up),
                20: (share(u, x - 1, 0), got_far.at[u, 1, 0], x_down),
                21: (share(u, x + 1, 0), got_far.at[u, 0, 0], x_up),
                22: (share(u, x - 1, 1), got_far.at[u, 1, 1], x_down),
                23: (share(u, x, theirs), got_pair.at[u], y_pair),
            }[k]
        return remote(u, k, src, dst, peer)

    def reduce_first(u):
        collect(u, x + 2)
        for k in (25,) if PAIRED[u] else (17, 18):
            reduce_copy(u, k).start()
        collect(u, x + 1)
        reduce_copy(u, 19).start()
        collect(u, x - 1)
        reduce_copy(u, 20).start()
        collect(u, x)

    def side(u):
        reduce_copy(u, 25).wait_recv()
        add_share(u, x + 2, y_lo, [lambda i: got_side[u, i]])
        reduce_copy(u, 17).start()
        reduce_copy(u, 18).start()

    def add_share(u, xx, yl, terms, start=0, count=own_blocks):
        first = row_at(xx, yl) * own_blocks

        def some(step, carry):
            for k in range(2):
                i = start + step * 2 + k
                total = partial[u, first + i].astype(F32)
                for term in terms:
                    total = total + term(i).astype(F32)
                partial[u, first + i] = total.astype(BF16)
            return carry

        lax.fori_loop(0, count // 2, some, 0)

    def second_a(u):
        reduce_copy(u, 17).wait_recv()
        if PAIRED[u]:
            add_share(u, x + 1, y_lo, [lambda i: got_opp[u, 0, i]], 0, half)
        else:
            add_share(u, x + 1, 0, [lambda i: got_opp[u, 0, i]])
        reduce_copy(u, 21).start()

    def second_b(u):
        reduce_copy(u, 18).wait_recv()
        if PAIRED[u]:
            add_share(u, x - 1, y_lo, [lambda i: got_opp[u, 1, i]], half, half)
        else:
            add_share(u, x - 1, 1, [lambda i: got_opp[u, 1, i]])
        reduce_copy(u, 22).start()

    def reduce_third(u):
        landed(u, 19, got_far.at[u])
        add_share(u, x, theirs, [lambda i: got_far[u, 0, theirs, i], lambda i: got_far[u, 1, theirs, i]])
        reduce_copy(u, 23).start()

    def out_copy(u):
        s, h = u // PARTS, u % PARTS
        return pltpu.make_async_copy(result.at[u], out_ref.at[s, 0, :, pl.ds(h * part, part), :], out_sem.at[u])

    def reduce_last(u):
        reduce_copy(u, 23).wait_recv()
        first = row_at(x, y_lo) * own_blocks

        def some(i, carry):
            total = partial[u, first + i].astype(F32) + got_far[u, 0, y_lo, i].astype(F32)
            total = total + got_far[u, 1, y_lo, i].astype(F32)
            result[u, i] = (total + got_pair[u, i].astype(F32)).astype(BF16)
            return carry

        lax.fori_loop(0, own_blocks, some, 0)
        out_copy(u).start()

    run = slots // 4
    tile_copies = [
        pltpu.make_async_copy(tile_ref.at[pl.ds(q * run, run)], tiles.at[pl.ds(q * run, run)], tile_sem.at[q])
        for q in range(4)
    ]

    loaded = []

    def product_run(q):
        def action(u):
            if q not in loaded:
                loaded.append(q)
                tile_copies[q].wait()
            products(u, q * run, run)

        return action

    actions = {f"p{q}": product_run(q) for q in range(4)}
    for action in (
        own_y, own_z, ring_own_a, ring_own_b, ring_other, half_a, half_b, opposite_own, opposite_other, gathered,
        reduce_first, side, second_a, second_b, reduce_third, reduce_last,
    ):
        actions[action.__name__] = action

    started = False
    for name, u in ORDER:
        if not started and name.startswith("ring"):
            started = True
            link_start()
            for copy in tile_copies:
                copy.start()
            sums[slots] = jnp.zeros(sums.shape[1:], F32)
            link_slots()
        actions[name](u)
    sent = tiles.at[pl.ds(0, 22 * own_blocks * part // pores)]
    for u in range(units):
        remote(u, 0, sent, sent, sibling).wait_send()
        out_copy(u).wait()


def shards(gradients, tile_blocks, tile_rows, tile_cols, tile_counts):
    sets, _, own_blocks, objectives, pores = gradients.shape
    slots = tile_blocks.shape[0]
    row_blocks = own_blocks * lax.axis_size("col")
    column_blocks = own_blocks * lax.axis_size("row")
    units, part = sets * PARTS, objectives // PARTS

    any_space = pl.BlockSpec(memory_space=pl.ANY)
    smem = pl.BlockSpec(memory_space=pltpu.SMEM)
    return pl.pallas_call(
        functools.partial(kernel, sets),
        out_shape=jax.ShapeDtypeStruct(gradients.shape, BF16),
        in_specs=[smem] + [any_space] * 4,
        out_specs=any_space,
        scratch_shapes=[pltpu.VMEM((row_blocks, part, pores), BF16) for _ in range(units)]
        + [
            pltpu.VMEM((slots, pores, pores), BF16),
            pltpu.VMEM((slots + 1, part, pores), F32),
            pltpu.VMEM((units, column_blocks, part, pores), BF16),
            pltpu.VMEM((units, 2, own_blocks, part, pores), BF16),
            pltpu.VMEM((units, 2, 2, own_blocks, part, pores), BF16),
            pltpu.VMEM((units, own_blocks, part, pores), BF16),
            pltpu.VMEM((units, own_blocks, part, pores), BF16),
            pltpu.VMEM((units, own_blocks, part, pores), BF16),
            pltpu.VMEM(((2 * slots + column_blocks) // LANES, LANES), jnp.int32),
            pltpu.VMEM(((2 * slots + column_blocks) // LANES, LANES), jnp.int32),
            pltpu.SMEM((2 * slots + column_blocks,), jnp.int32),
            pltpu.SMEM((slots,), jnp.int32),
            pltpu.SemaphoreType.DMA((units,)),
            pltpu.SemaphoreType.DMA((units, ARRIVALS)),
            pltpu.SemaphoreType.DMA((units,)),
            pltpu.SemaphoreType.DMA((4,)),
            pltpu.SemaphoreType.DMA((units,)),
            pltpu.SemaphoreType.DMA(((2 * slots + column_blocks) // LANES,)),
        ],
        compiler_params=pltpu.CompilerParams(
            collective_id=0, has_side_effects=True, vmem_limit_bytes=60 * 2**20
        ),
        cost_estimate=pl.CostEstimate(
            flops=2 * sets * slots * objectives * pores * pores, bytes_accessed=slots * pores * pores * 2, transcendentals=0
        ),
    )(tile_counts, tile_rows, tile_cols, gradients, tile_blocks)


def solution(mesh):
    in_specs = (
        P(None, "row", "col", None, None),
        P(("row", "col"), None, None),
        P(("row", "col")),
        P(("row", "col")),
        P(("row", "col")),
    )
    out_specs = P(None, "col", "row", None, None)
    return jax.shard_map(shards, mesh=mesh, in_specs=in_specs, out_specs=out_specs, check_vma=False)
```

time: 104 us -> 94.9 us (0.913)
  Pallas kernels: 101 us -> 92.1 us
    pallas_call x1, Pallas kernels: 101 us -> 92.1 us  [shards(): pl.pallas_call(functools.partial(kernel, sets), out_shape=jax.ShapeDtypeS...]
where the time goes in v3:
time: 94.9 us; the launch traced here: 94.8 us
  Pallas kernels  92.1 us (97%)
  local copies, waits for them, and re-layouts  2.06 us (2%)
    pallas_call x1, Pallas kernels, shards(): pl.pallas_call(functools.partial(kernel, sets), out_shape=jax.ShapeDtypeS...  92.1 us
    unnamed x1, local copies, waits for them, and re-layouts  2.06 us

profile of v3, /device:TPU:0, one launch (start us, length us, event | category | flops | bytes accessed | tf_op | source)
XLA Modules:
  0.0 94.8 jit_solution(11193783246789889961)
XLA Ops:
  0.7 92.1 %shard_map.55 = bf16[3,1,16,64,128]{4,3,2,1,0:T(8,128)(2,1)} custom-call(s32[1]{0:T(128)S(6)} %copy.7.count_ref, s32[384]{0:T(512)} %rows_ref.1, s32[384]{0:T(512)} %cols_ref.1, bf16[3,1,16,64,128]{4,3,2,1,0:T(8,128)(2,1)} %grad_ref.1, bf16[384,128,128]{2,1,0:T(8,128)(2,1)} %tile_ref.1), custom_call_target="tpu_custom_call" | custom-call | flops 2415919104 | bytes 12582912 | tf_op jit(solution)/shard_map/pallas_call | solution.py:383
  92.7 2.1 %copy.8 = bf16[3,1,16,64,128]{4,3,2,1,0:T(8,128)(2,1)} copy(bf16[3,1,16,64,128]{4,3,2,1,0:T(8,128)(2,1)} %shard_map.55) | data formatting | bytes 1572864

commit v4 on v3

--- a/solution.py
+++ b/solution.py
@@ -9,30 +9,30 @@
 
 MESH = pl.DeviceIdType.MESH
 PARTS = 2
-SIDE = (4, 4, 4, 4, 4, 4)
+SIDE = (3, 3, 3, 3, 3, 3)
 PAIRED = (False, False, True, True, True, True)
 ORDER = (
-    ("own_z", 1), ("own_y", 1), ("own_z", 2), ("ring_other", 1), ("own_y", 0), ("own_y", 2), ("ring_own_b", 1),
-    ("ring_own_a", 1), ("ring_own_b", 2), ("ring_own_a", 2), ("ring_other", 2), ("half_b", 1), ("half_a", 1),
-    ("opposite_own", 1), ("opposite_other", 1), ("own_z", 0), ("own_y", 4), ("opposite_own", 2), ("own_y", 3),
-    ("half_a", 2), ("half_b", 2), ("gathered", 1), ("p0", 1), ("ring_other", 0), ("p1", 1), ("p2", 1), ("own_z", 3),
-    ("own_y", 5), ("ring_own_a", 0), ("ring_own_b", 0), ("opposite_other", 2), ("p3", 1), ("reduce_first", 1),
-    ("gathered", 2), ("p0", 2), ("p1", 2), ("half_b", 0), ("half_a", 0), ("opposite_own", 0), ("ring_other", 3),
-    ("p2", 2), ("ring_own_a", 3), ("p3", 2), ("opposite_other", 0), ("ring_own_b", 3), ("reduce_first", 2),
-    ("own_z", 4), ("second_a", 1), ("second_b", 1), ("gathered", 0), ("p0", 0), ("half_b", 3), ("p1", 0),
-    ("opposite_own", 3), ("half_a", 3), ("ring_other", 4), ("side", 2), ("p2", 0), ("p3", 0), ("opposite_other", 3),
-    ("ring_own_b", 4), ("ring_own_a", 4), ("reduce_first", 0), ("own_z", 5), ("reduce_third", 1), ("gathered", 3),
-    ("p0", 3), ("second_b", 2), ("p1", 3), ("half_a", 4), ("opposite_own", 4), ("half_b", 4), ("second_a", 2),
-    ("ring_other", 5), ("p2", 3), ("p3", 3), ("opposite_other", 4), ("ring_own_a", 5), ("ring_own_b", 5),
-    ("reduce_first", 3), ("second_b", 0), ("second_a", 0), ("gathered", 4), ("p0", 4), ("half_b", 5), ("half_a", 5),
-    ("opposite_own", 5), ("p1", 4), ("p2", 4), ("side", 3), ("opposite_other", 5), ("p3", 4), ("reduce_first", 4),
-    ("gathered", 5), ("p0", 5), ("reduce_third", 2), ("second_b", 3), ("second_a", 3), ("p1", 5), ("p2", 5),
-    ("side", 4), ("p3", 5), ("reduce_first", 5), ("second_a", 4), ("reduce_third", 3), ("second_b", 4),
-    ("reduce_third", 0), ("side", 5), ("second_b", 5), ("second_a", 5), ("reduce_third", 4), ("reduce_last", 0),
-    ("reduce_last", 1), ("reduce_last", 2), ("reduce_third", 5), ("reduce_last", 4), ("reduce_last", 3),
-    ("reduce_last", 5),
+    ("own_z", 0), ("own_z", 1), ("own_y", 0), ("ring_other", 0), ("own_y", 1), ("ring_own_a", 0), ("own_y", 2),
+    ("ring_own_b", 0), ("ring_other", 1), ("opposite_own", 0), ("half_a", 0), ("half_b", 0), ("ring_own_a", 1),
+    ("ring_own_b", 1), ("opposite_other", 0), ("own_z", 2), ("half_a", 1), ("opposite_own", 1), ("half_b", 1),
+    ("gathered", 0), ("p0", 0), ("ring_other", 2), ("own_y", 4), ("p1", 0), ("p2", 0), ("opposite_other", 1),
+    ("ring_own_b", 2), ("ring_own_a", 2), ("reduce_first", 0), ("own_y", 5), ("own_z", 4), ("gathered", 1),
+    ("p0", 1), ("p1", 1), ("half_a", 2), ("half_b", 2), ("opposite_own", 2), ("ring_other", 4), ("p2", 1),
+    ("reduce_first", 1), ("ring_own_a", 4), ("own_y", 3), ("opposite_other", 2), ("ring_own_b", 4), ("second_a", 0),
+    ("second_b", 0), ("gathered", 2), ("own_z", 3), ("p0", 2), ("half_a", 4), ("half_b", 4), ("opposite_own", 4),
+    ("p1", 2), ("ring_other", 3), ("p2", 2), ("reduce_first", 2), ("opposite_other", 4), ("ring_own_a", 3),
+    ("ring_own_b", 3), ("second_b", 1), ("second_a", 1), ("gathered", 4), ("reduce_third", 0), ("own_z", 5),
+    ("p0", 4), ("p1", 4), ("half_b", 3), ("opposite_own", 3), ("half_a", 3), ("side", 2), ("ring_other", 5),
+    ("p2", 4), ("reduce_first", 4), ("opposite_other", 3), ("second_a", 2), ("ring_own_a", 5), ("ring_own_b", 5),
+    ("second_b", 2), ("gathered", 3), ("p0", 3), ("half_b", 5), ("half_a", 5), ("side", 4), ("opposite_own", 5),
+    ("p1", 3), ("p2", 3), ("reduce_first", 3), ("opposite_other", 5), ("second_a", 4), ("reduce_third", 2),
+    ("second_b", 4), ("gathered", 5), ("p0", 5), ("p1", 5), ("p2", 5), ("side", 3), ("reduce_first", 5),
+    ("second_a", 3), ("reduce_third", 4), ("side", 5), ("reduce_third", 1), ("second_b", 3), ("reduce_last", 0),
+    ("second_a", 5), ("second_b", 5), ("reduce_third", 3), ("reduce_third", 5), ("reduce_last", 4),
+    ("reduce_last", 2), ("reduce_last", 3), ("reduce_last", 1), ("reduce_last", 5),
 )
-UNROLL = 32
+UNROLL = 64
+RUNS = 3
 LANES = 128
 RECV = (0, 1, 2, 3, 4, 5, 6, 6, 7, 7, 3, 3, 3, 3, 3, 3, 3, 8, 9, 10, 10, 10, 10, 11, 7, 12)
 ARRIVALS = 13
@@ -215,10 +215,14 @@
 
     def products(u, first, count):
         def some(step, carry):
-            for k in range(UNROLL):
+            for k in range(0, UNROLL, 2):
                 t = first + step * UNROLL + k
-                picked = panels[u][link_ref[linked + t]]
-                sums[t] = sums[link_ref[t]] + jnp.dot(picked, tiles[t], preferred_element_type=F32)
+                x0, x1 = panels[u][link_ref[linked + t]], panels[u][link_ref[linked + t + 1]]
+                zero = jnp.zeros_like(x0)
+                left = jnp.concatenate([jnp.concatenate([x0, zero], 1), jnp.concatenate([zero, x1], 1)], 0)
+                both = jnp.dot(left, tiles[pl.ds(t, 2)].reshape(2 * pores, pores), preferred_element_type=F32)
+                sums[t] = sums[link_ref[t]] + both[:part]
+                sums[t + 1] = sums[link_ref[t + 1]] + both[part:]
             return carry
 
         lax.fori_loop(0, count // UNROLL, some, 0)
@@ -331,10 +335,10 @@
         lax.fori_loop(0, own_blocks, some, 0)
         out_copy(u).start()
 
-    run = slots // 4
+    run = slots // RUNS
     tile_copies = [
         pltpu.make_async_copy(tile_ref.at[pl.ds(q * run, run)], tiles.at[pl.ds(q * run, run)], tile_sem.at[q])
-        for q in range(4)
+        for q in range(RUNS)
     ]
 
     loaded = []
@@ -348,7 +352,7 @@
 
         return action
 
-    actions = {f"p{q}": product_run(q) for q in range(4)}
+    actions = {f"p{q}": product_run(q) for q in range(RUNS)}
     for action in (
         own_y, own_z, ring_own_a, ring_own_b, ring_other, half_a, half_b, opposite_own, opposite_other, gathered,
         reduce_first, side, second_a, second_b, reduce_third, reduce_last,
@@ -402,7 +406,7 @@
             pltpu.SemaphoreType.DMA((units,)),
             pltpu.SemaphoreType.DMA((units, ARRIVALS)),
             pltpu.SemaphoreType.DMA((units,)),
-            pltpu.SemaphoreType.DMA((4,)),
+            pltpu.SemaphoreType.DMA((RUNS,)),
             pltpu.SemaphoreType.DMA((units,)),
             pltpu.SemaphoreType.DMA(((2 * slots + column_blocks) // LANES,)),
         ],

time: 94.9 us -> 92.7 us (0.977)
  Pallas kernels: 92.1 us -> 89.8 us
    pallas_call x1, Pallas kernels: 92.1 us -> 89.8 us  [shards(): pl.pallas_call(functools.partial(kernel, sets), out_shape=jax.ShapeDtypeS...]
where the time goes in v4:
time: 92.7 us; the launch traced here: 92.6 us
  Pallas kernels  89.8 us (97%)
  local copies, waits for them, and re-layouts  2.06 us (2%)
    pallas_call x1, Pallas kernels, shards(): pl.pallas_call(functools.partial(kernel, sets), out_shape=jax.ShapeDtypeS...  89.8 us
    unnamed x1, local copies, waits for them, and re-layouts  2.06 us

profile of v4, /device:TPU:0, one launch (start us, length us, event | category | flops | bytes accessed | tf_op | source)
XLA Modules:
  0.0 92.6 jit_solution(13123207112760163326)
XLA Ops:
  0.7 89.8 %shard_map.55 = bf16[3,1,16,64,128]{4,3,2,1,0:T(8,128)(2,1)} custom-call(s32[1]{0:T(128)S(6)} %copy.7.count_ref, s32[384]{0:T(512)} %rows_ref.1, s32[384]{0:T(512)} %cols_ref.1, bf16[3,1,16,64,128]{4,3,2,1,0:T(8,128)(2,1)} %grad_ref.1, bf16[384,128,128]{2,1,0:T(8,128)(2,1)} %tile_ref.1), custom_call_target="tpu_custom_call" | custom-call | flops 2415919104 | bytes 12582912 | tf_op jit(solution)/shard_map/pallas_call | solution.py:387
  90.5 2.1 %copy.8 = bf16[3,1,16,64,128]{4,3,2,1,0:T(8,128)(2,1)} copy(bf16[3,1,16,64,128]{4,3,2,1,0:T(8,128)(2,1)} %shard_map.55) | data formatting | bytes 1572864

commit v5 on v4

--- a/solution.py
+++ b/solution.py
@@ -12,24 +12,24 @@
 SIDE = (3, 3, 3, 3, 3, 3)
 PAIRED = (False, False, True, True, True, True)
 ORDER = (
-    ("own_z", 0), ("own_z", 1), ("own_y", 0), ("ring_other", 0), ("own_y", 1), ("ring_own_a", 0), ("own_y", 2),
-    ("ring_own_b", 0), ("ring_other", 1), ("opposite_own", 0), ("half_a", 0), ("half_b", 0), ("ring_own_a", 1),
-    ("ring_own_b", 1), ("opposite_other", 0), ("own_z", 2), ("half_a", 1), ("opposite_own", 1), ("half_b", 1),
-    ("gathered", 0), ("p0", 0), ("ring_other", 2), ("own_y", 4), ("p1", 0), ("p2", 0), ("opposite_other", 1),
-    ("ring_own_b", 2), ("ring_own_a", 2), ("reduce_first", 0), ("own_y", 5), ("own_z", 4), ("gathered", 1),
-    ("p0", 1), ("p1", 1), ("half_a", 2), ("half_b", 2), ("opposite_own", 2), ("ring_other", 4), ("p2", 1),
-    ("reduce_first", 1), ("ring_own_a", 4), ("own_y", 3), ("opposite_other", 2), ("ring_own_b", 4), ("second_a", 0),
-    ("second_b", 0), ("gathered", 2), ("own_z", 3), ("p0", 2), ("half_a", 4), ("half_b", 4), ("opposite_own", 4),
-    ("p1", 2), ("ring_other", 3), ("p2", 2), ("reduce_first", 2), ("opposite_other", 4), ("ring_own_a", 3),
-    ("ring_own_b", 3), ("second_b", 1), ("second_a", 1), ("gathered", 4), ("reduce_third", 0), ("own_z", 5),
-    ("p0", 4), ("p1", 4), ("half_b", 3), ("opposite_own", 3), ("half_a", 3), ("side", 2), ("ring_other", 5),
-    ("p2", 4), ("reduce_first", 4), ("opposite_other", 3), ("second_a", 2), ("ring_own_a", 5), ("ring_own_b", 5),
-    ("second_b", 2), ("gathered", 3), ("p0", 3), ("half_b", 5), ("half_a", 5), ("side", 4), ("opposite_own", 5),
-    ("p1", 3), ("p2", 3), ("reduce_first", 3), ("opposite_other", 5), ("second_a", 4), ("reduce_third", 2),
-    ("second_b", 4), ("gathered", 5), ("p0", 5), ("p1", 5), ("p2", 5), ("side", 3), ("reduce_first", 5),
-    ("second_a", 3), ("reduce_third", 4), ("side", 5), ("reduce_third", 1), ("second_b", 3), ("reduce_last", 0),
-    ("second_a", 5), ("second_b", 5), ("reduce_third", 3), ("reduce_third", 5), ("reduce_last", 4),
-    ("reduce_last", 2), ("reduce_last", 3), ("reduce_last", 1), ("reduce_last", 5),
+    ("own_z", 1), ("own_y", 1), ("own_z", 2), ("ring_other", 1), ("own_y", 2), ("ring_own_a", 1), ("ring_own_b", 1),
+    ("ring_other", 2), ("ring_own_b", 2), ("ring_own_a", 2), ("own_y", 5), ("opposite_own", 1), ("half_b", 1),
+    ("half_a", 1), ("opposite_own", 2), ("own_z", 5), ("opposite_other", 1), ("own_y", 3), ("half_b", 2),
+    ("half_a", 2), ("own_y", 4), ("ring_other", 5), ("gathered", 1), ("p0", 1), ("p1", 1), ("opposite_other", 2),
+    ("own_y", 0), ("ring_own_a", 5), ("ring_own_b", 5), ("p2", 1), ("own_z", 4), ("reduce_first", 1),
+    ("gathered", 2), ("half_b", 5), ("p0", 2), ("half_a", 5), ("ring_other", 4), ("opposite_own", 5), ("p1", 2),
+    ("p2", 2), ("reduce_first", 2), ("ring_own_a", 4), ("opposite_other", 5), ("ring_own_b", 4), ("second_b", 1),
+    ("second_a", 1), ("own_z", 3), ("gathered", 5), ("p0", 5), ("half_b", 4), ("half_a", 4), ("ring_other", 3),
+    ("opposite_own", 4), ("side", 2), ("p1", 5), ("p2", 5), ("reduce_first", 5), ("opposite_other", 4),
+    ("ring_own_a", 3), ("ring_own_b", 3), ("second_a", 2), ("second_b", 2), ("gathered", 4), ("own_z", 0), ("p0", 4),
+    ("half_b", 3), ("half_a", 3), ("ring_other", 0), ("side", 5), ("opposite_own", 3), ("p1", 4), ("p2", 4),
+    ("reduce_first", 4), ("opposite_other", 3), ("second_a", 5), ("second_b", 5), ("ring_own_a", 0),
+    ("ring_own_b", 0), ("gathered", 3), ("p0", 3), ("p1", 3), ("half_a", 0), ("opposite_own", 0), ("half_b", 0),
+    ("side", 4), ("p2", 3), ("reduce_first", 3), ("opposite_other", 0), ("second_a", 4), ("reduce_third", 5),
+    ("second_b", 4), ("reduce_third", 1), ("gathered", 0), ("p0", 0), ("p1", 0), ("side", 3), ("p2", 0),
+    ("reduce_first", 0), ("reduce_last", 5), ("reduce_third", 4), ("second_a", 3), ("reduce_last", 1),
+    ("reduce_third", 2), ("second_b", 3), ("second_a", 0), ("second_b", 0), ("reduce_third", 3), ("reduce_third", 0),
+    ("reduce_last", 3), ("reduce_last", 4), ("reduce_last", 2), ("reduce_last", 0),
 )
 UNROLL = 64
 RUNS = 3

time: 92.7 us -> 92.3 us (level)
  Pallas kernels: 89.8 us -> 88.5 us
    pallas_call x1, Pallas kernels: 89.8 us -> 88.5 us  [shards(): pl.pallas_call(functools.partial(kernel, sets), out_shape=jax.ShapeDtypeS...]
where the time goes in v5:
time: 92.3 us; the launch traced here: 91.3 us
  Pallas kernels  88.5 us (96%)
  local copies, waits for them, and re-layouts  2.06 us (2%)
    pallas_call x1, Pallas kernels, shards(): pl.pallas_call(functools.partial(kernel, sets), out_shape=jax.ShapeDtypeS...  88.5 us
    unnamed x1, local copies, waits for them, and re-layouts  2.06 us

profile of v5, /device:TPU:0, one launch (start us, length us, event | category | flops | bytes accessed | tf_op | source)
XLA Modules:
  0.0 91.3 jit_solution(5162602165279118584)
XLA Ops:
  0.7 88.5 %shard_map.55 = bf16[3,1,16,64,128]{4,3,2,1,0:T(8,128)(2,1)} custom-call(s32[1]{0:T(128)S(6)} %copy.7.count_ref, s32[384]{0:T(512)} %rows_ref.1, s32[384]{0:T(512)} %cols_ref.1, bf16[3,1,16,64,128]{4,3,2,1,0:T(8,128)(2,1)} %grad_ref.1, bf16[384,128,128]{2,1,0:T(8,128)(2,1)} %tile_ref.1), custom_call_target="tpu_custom_call" | custom-call | flops 2415919104 | bytes 12582912 | tf_op jit(solution)/shard_map/pallas_call | solution.py:387
  89.2 2.1 %copy.8 = bf16[3,1,16,64,128]{4,3,2,1,0:T(8,128)(2,1)} copy(bf16[3,1,16,64,128]{4,3,2,1,0:T(8,128)(2,1)} %shard_map.55) | data formatting | bytes 1572864
